TPU v7x, 32 devices: a whole 2x2x4 slice. The times are simulated.
32 devices in a mesh: dp: 2 (over core), cent: 16 (over z, y, x).
Axes of the slice: x: 2, y: 2, z: 4, core: 2. Of those that a mesh axis runs over, the one named last changes fastest.
Arguments:
- points: bfloat16 [4096, 768], P(('dp', 'cent')), may hold values from -16 to 16
- centroids: float32 [32768, 768], P(('dp', 'cent')), may hold values from -1.5 to 1.5
Outputs:
- new_centroids: float32 [32768, 768], P(('dp', 'cent'))
- log_total: float32 [4096], P(('dp', 'cent'))
All inputs are finite; a program needn't handle non-finite values.
Results may differ from a plain program's by a relative error of at most 0.0088.
Values may be sent and summed in bfloat16 or wider, within the bound.
A program may use at most 128 MiB of HBM per device.

v0:
```python
import math

import jax
import jax.numpy as jnp
from jax import lax
from jax.sharding import PartitionSpec as P

BLOCKS = 2


def score_block(members, cent_block, score_scale):
    sq_norm = jnp.sum(jnp.square(cent_block.astype(jnp.float32)), axis=1)
    products = lax.dot_general(
        members, cent_block, (((1,), (1,)), ((), ())), preferred_element_type=jnp.float32
    )
    return (2.0 * products - sq_norm[None, :]) * score_scale


def fold_stats(running, scores):
    old_max, old_sum = running
    new_max = jnp.maximum(old_max, jnp.max(scores, axis=1))
    new_sum = old_sum * jnp.exp(old_max - new_max) + jnp.sum(
        jnp.exp(scores - new_max[:, None]), axis=1
    )
    return (new_max, new_sum)


def on_device(points, centroids):
    feature_width = centroids.shape[1]
    own_rows = centroids.shape[0]
    dp_count = lax.axis_size("dp")
    score_scale = 7.0 / math.sqrt(feature_width)
    copies = centroids.astype(jnp.bfloat16)
    members = lax.all_gather(points, "cent", axis=0, tiled=True)
    member_rows = members.shape[0]
    start = (jnp.full((member_rows,), -1e30, jnp.float32), jnp.zeros((member_rows,), jnp.float32))
    part_rows = own_rows // BLOCKS
    gathered = lax.all_gather(copies, "dp", axis=0, tiled=True)
    running = start
    block_span = gathered.shape[0] // BLOCKS
    for index_j in range(BLOCKS):
        running = fold_stats(
            running,
            score_block(
                members, gathered[index_j * block_span : (index_j + 1) * block_span], score_scale
            ),
        )
    local_max, local_sum = running
    global_max = lax.pmax(local_max.astype(jnp.bfloat16), "cent").astype(local_max.dtype)
    global_sum = lax.psum(local_sum * jnp.exp(local_max - global_max), "cent")
    log_total = global_max + jnp.log(global_sum)
    arranged = gathered.reshape(dp_count, BLOCKS, part_rows, feature_width)
    sum_parts = []
    count_parts = []
    for index_j in range(BLOCKS):
        cent_block = arranged[:, index_j].reshape(dp_count * part_rows, feature_width)
        scores = score_block(members, cent_block, score_scale)
        weights = jnp.exp(scores - log_total[:, None]).astype(jnp.bfloat16)
        partial_sums = lax.dot_general(
            weights, members, (((0,), (0,)), ((), ())), preferred_element_type=jnp.float32
        )
        counts = jnp.sum(weights, axis=0, dtype=jnp.float32)
        owned_sums, owned_counts = (
            lax.psum_scatter(partial_sums, "dp", scatter_dimension=0, tiled=True),
            lax.psum_scatter(counts, "dp", scatter_dimension=0, tiled=True),
        )
        sum_parts.append(owned_sums)
        count_parts.append(owned_counts)
    own_sums = jnp.concatenate(sum_parts, axis=0)
    own_counts = jnp.concatenate(count_parts, axis=0)
    new_centroids = (own_sums + centroids) / (own_counts[:, None] + 1.0)
    own_points = points.shape[0]
    own_total = lax.dynamic_slice_in_dim(log_total, lax.axis_index("cent") * own_points, own_points)
    return (new_centroids, own_total)


def solution(mesh):
    placed = (P(("dp", "cent"), None), P(("dp", "cent"), None))
    return jax.shard_map(
        on_device,
        mesh=mesh,
        in_specs=placed,
        out_specs=(P(("dp", "cent"), None), P(("dp", "cent"))),
        check_vma=False,
    )
```

profile of v0, /device:TPU:0, one launch (start us, length us, event | category | flops | bytes accessed | tf_op | source)
XLA Modules:
  0.0 242.2 jit_solution(846366782806502446)
XLA Ops:
  7.2 0.0 all-gather.5.cloned.1.call-start
  7.2 3.2 %convert_element_type.35 = bf16[1024,768]{1,0:T(8,128)(2,1)} convert(f32[1024,768]{1,0:T(8,128)} %param.3) | non-fusion elementwise | flops 786432 | bytes 4718592 | tf_op jit(solution)/shard_map/convert_element_type | solution.py:33
  10.4 0.0 all-gather.5.cloned.1.call-update
  10.4 0.0 all-gather.3.cloned.1.call-start
  10.5 0.7 all-gather.3.cloned.1.call-update
  11.2 0.0 reduce-scatter.5.cloned.1.call-start
  11.2 14.2 %all-gather.5.cloned.1.call-done = bf16[2048,768]{1,0:T(8,128)(2,1)} async-done(((bf16[1024,768]{1,0:T(8,128)(2,1)}), bf16[2048,768]{1,0:T(8,128)(2,1)}) %all-gather.5.cloned.1.call-update) | async-done | bytes 3145744 | tf_op jit(solution)/shard_map/all_gather | solution.py:38
  25.4 0.0 copy-start
  25.4 2.7 %multiply_reduce_fusion.3 = (f32[2,512]{1,0:T(2,128)S(1)}, f32[2,512]{1,0:T(2,128)S(1)}) fusion(bf16[2,2,512,768]{3,2,1,0:T(8,128)(2,1)} %bitcast.18), kind=kLoop, calls=%fused_computation.15 | loop fusion | flops 4716544 | bytes 3153920 | tf_op jit(solution)/shard_map/reduce_sum | solution.py:12
  28.1 0.1 copy-done
  28.2 0.7 multiply_reduce_fusion.2
  28.9 1.9 fusion.12
  30.8 66.7 %all-gather.3.cloned.1.call-done = bf16[2048,768]{1,0:T(8,128)(2,1)} async-done(((bf16[128,768]{1,0:T(8,128)(2,1)}), bf16[2048,768]{1,0:T(8,128)(2,1)}) %all-gather.3.cloned.1.call-update) | async-done | bytes 3145744 | tf_op jit(solution)/shard_map/all_gather | solution.py:34
  97.5 0.0 copy-start.4
  97.5 8.2 %fusion.1 = (f32[2048]{0:T(1024)S(1)}, f32[2048,1024]{1,0:T(8,128)}) fusion(f32[1024]{0:T(1024)S(1)} %get-tuple-element.5, bf16[2048,768]{1,0:T(8,128)(2,1)} %all-gather.3.cloned.1.call-done, bf16[2048,768]{1,0:T(8,128)(2,1)S(1)} %copy-done), kind=kOutput, calls=%fused_computation.9 | convolution fusion | flops 3229612032 | bytes 13119488 | tf_op jit(solution)/shard_map/dot_general | solution.py:13
  105.7 0.0 copy-done.4
  105.7 6.3 %fusion = (f32[2048]{0:T(1024)S(1)}, f32[2048,1024]{1,0:T(8,128)}) fusion(f32[1024]{0:T(1024)S(1)} %get-tuple-element.4, bf16[2048,768]{1,0:T(8,128)(2,1)S(1)} %copy-done.4, bf16[2048,768]{1,0:T(8,128)(2,1)S(1)} %copy-done), kind=kOutput, calls=%fused_computation.8 | convolution fusion | flops 3229612032 | bytes 13119488 | tf_op jit(solution)/shard_map/dot_general | solution.py:13
  112.0 39.3 %pmax.7 = bf16[2048]{0:T(1024)(128)(2,1)S(1)} all-reduce(bf16[2048]{0:T(1024)(128)(2,1)S(1)} %get-tuple-element.8), channel_id=1, replica_groups=mesh['dp'=2,'cent'=16] {'cent'}, use_global_device_ids=true, to_apply=%region_5.0 | all-reduce | flops 2048 | bytes 8192 | tf_op jit(solution)/shard_map/pmax | solution.py:49
  151.3 0.0 copy-start.3
  151.3 8.0 %exponential_reduce_fusion = (f32[2048]{0:T(1024)S(1)}, f32[2048]{0:T(1024)S(1)}) fusion(f32[2048,1024]{1,0:T(8,128)} %get-tuple-element.14, f32[2048]{0:T(1024)S(1)} %get-tuple-element.9, f32[1024]{0:T(1024)S(1)} %get-tuple-element.5, f32[2048]{0:T(1024)S(1)} %get-tuple-element.12, f32[1024]{0:T(1024)S(1)} %get-tuple-element.4, ...), kind=kLoop, calls=%fused_computation.4 | loop fusion | flops 20967424 | bytes 16818176 | tf_op jit(solution)/shard_map/reduce_sum | solution.py:22
  159.4 37.3 %psum.7 = f32[2048]{0:T(1024)S(1)} all-reduce(f32[2048]{0:T(1024)S(1)} %fusion.8), channel_id=1, replica_groups=mesh['dp'=2,'cent'=16] {'cent'}, use_global_device_ids=true, to_apply=%region_8.0 | all-reduce | flops 2048 | bytes 16384 | tf_op jit(solution)/shard_map/psum | solution.py:50
  196.8 0.0 copy-done.3
  196.8 0.0 copy-start.5
  196.8 6.6 %convert_reduce_fusion = (f32[1024]{0:T(1024)S(1)}, bf16[2048,1024]{1,0:T(8,128)(2,1)S(1)}) fusion(f32[2048]{0:T(1024)S(1)} %convert_add_fusion, f32[1024]{0:T(1024)S(1)} %bitcast.24, bf16[2048,768]{1,0:T(8,128)(2,1)} %all-gather.3.cloned.1.call-done, bf16[1024,768]{1,0:T(8,128)(2,1)S(1)} %bitcast.21), kind=kOutput, calls=%fused_computation | convolution fusion | flops 3235904512 | bytes 8929280 | tf_op jit(solution)/shard_map/dot_general | solution.py:13
  203.4 0.0 copy-done.5
  203.4 5.3 %fusion.14 = f32[1024,768]{1,0:T(8,128)} fusion(bf16[2048,1024]{1,0:T(8,128)(2,1)S(1)} %get-tuple-element.18, bf16[2048,768]{1,0:T(8,128)(2,1)S(1)} %copy-done.5), kind=kOutput, calls=%fused_computation.30 | convolution fusion | flops 3221225472 | bytes 10485760 | tf_op jit(solution)/shard_map/dot_general | solution.py:59
  208.7 0.0 copy-start.2
  208.7 0.0 reduce-scatter.5.cloned.1.call-update
  208.7 0.3 reduce-scatter.3.cloned.1.call-start
  209.0 1.1 copy-done.2
  210.1 0.0 copy-start.6
  210.1 6.6 %convert_reduce_fusion.1 = (f32[1024]{0:T(1024)S(1)}, bf16[2048,1024]{1,0:T(8,128)(2,1)S(1)}) fusion(f32[2048]{0:T(1024)S(1)} %convert_add_fusion, f32[1024]{0:T(1024)S(1)} %bitcast.25, bf16[2048,768]{1,0:T(8,128)(2,1)} %all-gather.3.cloned.1.call-done, bf16[1024,768]{1,0:T(8,128)(2,1)S(1)} %bitcast.20), kind=kOutput, calls=%fused_computation.1 | convolution fusion | flops 3235904512 | bytes 8929280 | tf_op jit(solution)/shard_map/dot_general | solution.py:13
  216.7 0.0 copy-done.6
  216.7 5.3 %fusion.13 = f32[1024,768]{1,0:T(8,128)} fusion(bf16[2048,1024]{1,0:T(8,128)(2,1)S(1)} %get-tuple-element.20, bf16[2048,768]{1,0:T(8,128)(2,1)S(1)} %copy-done.6), kind=kOutput, calls=%fused_computation.29 | convolution fusion | flops 3221225472 | bytes 10485760 | tf_op jit(solution)/shard_map/dot_general | solution.py:59
  222.0 0.0 copy-start.7
  222.0 0.0 copy-start.1
  222.0 0.0 reduce-scatter.3.cloned.1.call-update
  222.1 0.6 copy-done.7
  222.7 0.6 dynamic-slice
  223.9 2.5 %all-reduce.2 = (f32[1024]{0:T(1024)S(1)}, f32[1024]{0:T(1024)S(1)}) all-reduce(f32[1024]{0:T(1024)S(1)} %get-tuple-element.17, f32[1024]{0:T(1024)S(1)} %get-tuple-element.19), channel_id=5, replica_groups=mesh['dp'=2,'cent'=16] {'dp'}, use_global_device_ids=true, to_apply=%region_15.0.clone | all-reduce | flops 2048 | bytes 16384
  226.4 0.1 dynamic-slice.3
  226.5 0.1 dynamic-slice.1
  226.6 0.6 dynamic_slice.3
  227.2 0.0 reduce-scatter.5.cloned.1.call-done
  227.2 4.6 %reduce-scatter.3.cloned.1.call-done = f32[512,768]{1,0:T(8,128)} async-done(((f32[1024,768]{1,0:T(8,128)}), f32[512,768]{1,0:T(8,128)}) %reduce-scatter.3.cloned.1.call-update) | async-done | bytes 1572880 | tf_op jit(solution)/shard_map/reduce_scatter | solution.py:64
  231.8 0.0 copy-done.1
  231.8 3.9 %fusion.2 = f32[1024,768]{1,0:T(8,128)} fusion(f32[1024,768]{1,0:T(8,128)S(1)} %copy-done.1, f32[512,768]{1,0:T(8,128)} %reduce-scatter.5.cloned.1.call-done, f32[512,768]{1,0:T(8,128)} %reduce-scatter.3.cloned.1.call-done, f32[1024]{0:T(1024)S(1)} %maximum_add_fusion.1), kind=kLoop, calls=%fused_computation.11 | loop fusion | flops 2359296 | bytes 9441280 | tf_op jit(solution)/shard_map/div | solution.py:71
  (6 shorter events, 0.0 us)
Async XLA Ops:
  7.2 18.2 %all-gather.5.cloned.1.call-start = ((), (), s32[]{:S(2)}) async-start(), calls=%async_computation.3 | async-start | bytes 4718592 | tf_op jit(solution)/shard_map/all_gather | solution.py:38
  10.4 87.1 %all-gather.3.cloned.1.call-start = ((), (), s32[]{:S(2)}) async-start(), calls=%async_computation.2 | async-start | bytes 3342336 | tf_op jit(solution)/shard_map/all_gather | solution.py:34
  11.2 216.0 %reduce-scatter.5.cloned.1.call-start = ((), (), s32[]{:S(2)}) async-start(), calls=%async_computation.5 | async-start | bytes 4718592 | tf_op jit(solution)/shard_map/reduce_scatter | solution.py:64
  25.4 2.8 %copy-start = (bf16[2048,768]{1,0:T(8,128)(2,1)S(1)}, bf16[2048,768]{1,0:T(8,128)(2,1)}, u32[]{:S(2)}) copy-start(bf16[2048,768]{1,0:T(8,128)(2,1)} %all-gather.5.cloned.1.call-done) | copy-start | bytes 9437188
  97.5 8.2 %copy-start.4 = (bf16[2048,768]{1,0:T(8,128)(2,1)S(1)}, bf16[2048,768]{1,0:T(8,128)(2,1)}, u32[]{:S(2)}) copy-start(bf16[2048,768]{1,0:T(8,128)(2,1)} %all-gather.3.cloned.1.call-done) | copy-start | bytes 9437188
  151.3 45.4 %copy-start.3 = (bf16[2,1,512,768]{3,2,1,0:T(8,128)(2,1)S(1)}, bf16[2,1,512,768]{3,2,1,0:T(8,128)(2,1)}, u32[]{:S(2)}) copy-start(bf16[2,1,512,768]{3,2,1,0:T(8,128)(2,1)} %get-tuple-element.11) | copy-start | bytes 4718596
  196.8 6.6 %copy-start.5 = (bf16[2048,768]{1,0:T(8,128)(2,1)S(1)}, bf16[2048,768]{1,0:T(8,128)(2,1)}, u32[]{:S(2)}) copy-start(bf16[2048,768]{1,0:T(8,128)(2,1)} %all-gather.3.cloned.1.call-done) | copy-start | bytes 9437188
  208.7 1.4 copy-start.2
  208.7 23.0 %reduce-scatter.3.cloned.1.call-start = ((), (), s32[]{:S(2)}) async-start(), calls=%async_computation.4 | async-start | bytes 4718592 | tf_op jit(solution)/shard_map/reduce_scatter | solution.py:64
  210.1 6.6 %copy-start.6 = (bf16[2048,768]{1,0:T(8,128)(2,1)S(1)}, bf16[2048,768]{1,0:T(8,128)(2,1)}, u32[]{:S(2)}) copy-start(bf16[2048,768]{1,0:T(8,128)(2,1)} %all-gather.3.cloned.1.call-done) | copy-start | bytes 9437188
  222.0 0.7 copy-start.7
  222.0 9.7 %copy-start.1 = (f32[1024,768]{1,0:T(8,128)S(1)}, f32[1024,768]{1,0:T(8,128)}, u32[]{:S(2)}) copy-start(f32[1024,768]{1,0:T(8,128)} %param.3) | copy-start | bytes 9437188
Sparse Core Ops, SparseCore 0:
  10.5 14.8 all-gather.4
  28.2 69.2 all-gather.2
  208.8 8.5 reduce-scatter.4
  222.2 9.5 reduce-scatter.2
where the time goes:
time: 242 us
  waiting for transfers between devices  86.2 us (36%)
  blocking collectives  79.1 us (33%)
  matrix products  38.3 us (16%)
  other arithmetic  18.6 us (8%)
  between operations  14.5 us (6%)
  local copies, waits for them, and re-layouts  5.03 us (2%)
    all_gather x1, waiting for transfers between devices, on_device(): members = lax.all_gather(points, 'cent', axis=0, tiled=True)  66.7 us
    pmax x1, blocking collectives, on_device(): lax.pmax(local_max.astype(jnp.bfloat16), 'cent').astype(local_max.dtype)  39.3 us
    psum x1, blocking collectives, on_device(): global_sum = lax.psum(local_sum * jnp.exp(local_max - global_max), 'cent')  37.3 us
    dot_general x4, matrix products, score_block(): lax.dot_general(members, cent_block, (((1,), (1,)), ((), ())), preferred_...  27.7 us
    all_gather x1, waiting for transfers between devices, on_device(): gathered = lax.all_gather(copies, 'dp', axis=0, tiled=True)  14.2 us
    dot_general x2, matrix products, on_device(): lax.dot_general(weights, members, (((0,), (0,)), ((), ())), preferred_ele...  10.7 us
    reduce_sum x1, other arithmetic, fold_stats(): jnp.sum(jnp.exp(scores - new_max[:, None]), axis=1)  8.04 us
  transfers between devices with their start and end apart: 4, of which 3 were waited for; matrix products, arithmetic and copies ran while one was open for 8% of the time, Pallas kernels for 0%

commit v1 on v0

v1 whole, which is shorter than its diff:
```python
import functools
import math

import jax
import jax.numpy as jnp
from jax import lax
from jax.experimental import pallas as pl
from jax.experimental.pallas import tpu as pltpu
from jax.sharding import PartitionSpec as P

MESH = pl.DeviceIdType.MESH
LOG2E = 1.4426950408889634
LN2 = 0.6931471805599453
Z_AXIS, Y_AXIS, X_AXIS = 0, 1, 2
SHARES = (
    (0.5, (Z_AXIS, X_AXIS, Y_AXIS)),
    (0.5, (Z_AXIS, Y_AXIS, X_AXIS)),
)
SEND_DEPTH = 16
NEAREST = (
    (0, 0, 0), (0, 0, 1), (0, 1, 0), (1, 0, 0), (0, 1, 1), (1, 0, 1), (1, 1, 0), (2, 0, 0),
    (1, 1, 1), (2, 0, 1), (2, 1, 0), (3, 0, 0), (2, 1, 1), (3, 0, 1), (3, 1, 0), (3, 1, 1),
)


def chip_grid(chips):
    sizes = [1, 1, 1]
    axis = 0
    order = (Z_AXIS, Y_AXIS, X_AXIS)
    left = chips
    if chips >= 16:
        sizes[0] = 4
        left //= 4
    while left > 1:
        sizes[order[axis % 3]] *= 2 if (chips < 16 or axis % 3) else 1
        left = chips // (sizes[0] * sizes[1] * sizes[2])
        axis += 1
    return tuple(sizes)


def row_parts(rows):
    parts, first = [], 0
    for index, (share, order) in enumerate(SHARES):
        last = rows if index == len(SHARES) - 1 else first + int(share * rows) // 16 * 16
        parts.append((first, last - first, order))
        first = last
    return parts


def ranked(rank, at, size):
    if size == 1:
        return at * 0
    if size == 2:
        return lax.rem(at + rank, 2)
    low = jnp.where(at < 2, at, 3 - at)
    place = jnp.where(low == 0, rank, jnp.where(rank == 3, 3, lax.rem(rank + 1, 3)))
    return jnp.where(at < 2, place, 3 - place)


def source_of(step, at, grid):
    nz, ny, nx = grid
    if grid == (4, 2, 2):
        ranks = []
        for axis in range(3):
            value = jnp.int32(NEAREST[0][axis])
            for index in range(1, len(NEAREST)):
                value = jnp.where(step == index, NEAREST[index][axis], value)
            ranks.append(value)
    else:
        ranks = [step // (ny * nx), (step // nx) % ny, step % nx]
    return [ranked(rank, place, size) for rank, place, size in zip(ranks, at, grid)]


def kernel(
    grid, parts, alpha, chunk,
    points_ref, cent_hbm, out_hbm, total_ref,
    xbuf, acc, copies, norms, ebuf, weights, counts, local_max,
    stat_out, stat_in, totals,
    load_sem, store_sem, send_sem, recv_sem, side_send, side_recv,
    stat_send, stat_recv, total_send, total_recv,
):
    nz, ny, nx = grid
    chips = nz * ny * nx
    devices = 2 * chips
    core = lax.axis_index("dp")
    chip = lax.axis_index("cent")
    me = chip * 2 + core
    at = [chip // (ny * nx), (chip // nx) % ny, chip % nx]
    strides = (ny * nx, nx, 1)
    own_rows = copies.shape[0]

    load = pltpu.make_async_copy(cent_hbm, acc, load_sem)
    load.start()

    barrier = pltpu.get_barrier_semaphore()

    def greet(index, carry):
        other = lax.rem(me + index, devices)
        pl.semaphore_signal(
            barrier, inc=1, device_id=(lax.rem(other, 2), other // 2), device_id_type=MESH
        )
        return carry

    lax.fori_loop(1, devices, greet, 0)
    xbuf[chip, core] = points_ref[...]
    pl.semaphore_wait(barrier, devices - 1)

    def part_copy(source, slot, link, part, target):
        first, rows, _ = parts[part]
        piece = xbuf.at[source, core, pl.ds(first, rows)]
        return pltpu.make_async_remote_copy(
            src_ref=piece,
            dst_ref=piece,
            send_sem=send_sem.at[slot, link],
            recv_sem=recv_sem.at[source, part],
            device_id=(core, target),
            device_id_type=MESH,
        )

    def side_copy(source):
        return pltpu.make_async_remote_copy(
            src_ref=xbuf.at[source, core],
            dst_ref=xbuf.at[source, core],
            send_sem=side_send.at[source],
            recv_sem=side_recv.at[source],
            device_id=(1 - core, chip),
            device_id_type=MESH,
        )

    def index_of(place):
        return place[0] * strides[0] + place[1] * strides[1] + place[2]

    def forwards(step, act):
        place = source_of(step, at, grid)
        source = index_of(place)
        slot = lax.rem(step, SEND_DEPTH)
        link = 0
        for part, (_, _, order) in enumerate(parts):
            for position, axis in enumerate(order):
                if grid[axis] == 1:
                    continue
                clear = None
                for later in order[position + 1 :]:
                    if grid[later] > 1:
                        same = place[later] == at[later]
                        clear = same if clear is None else jnp.logical_and(clear, same)
                if grid[axis] == 2:
                    options = [(place[axis] == at[axis], (1 - 2 * at[axis]) * strides[axis])]
                else:
                    options = [
                        (
                            jnp.logical_and(place[axis] <= at[axis], at[axis] < grid[axis] - 1),
                            strides[axis],
                        ),
                        (
                            jnp.logical_and(place[axis] >= at[axis], at[axis] > 0),
                            -strides[axis],
                        ),
                    ]
                for condition, shift in options:
                    if clear is not None:
                        condition = jnp.logical_and(condition, clear)

                    @pl.when(condition)
                    def _(link=link, part=part, shift=shift):
                        act(part_copy(source, slot, link, part, chip + shift))

                    link += 1
        return source

    def stat_copy(source, half):
        return pltpu.make_async_remote_copy(
            src_ref=stat_out.at[source * 2 + half],
            dst_ref=stat_in.at[me],
            send_sem=stat_send,
            recv_sem=stat_recv,
            device_id=(half, source),
            device_id_type=MESH,
        )

    def score(source):
        block = xbuf[source].reshape(2 * xbuf.shape[2], xbuf.shape[3])
        products = lax.dot_general(
            copies[...], block, (((1,), (1,)), ((), ())), preferred_element_type=jnp.float32
        )
        scores = products * (2.0 * alpha) - norms[...]
        largest = jnp.max(scores, axis=0, keepdims=True)
        terms = jnp.exp2(scores - largest)
        ebuf[source] = terms
        summed = jnp.sum(terms, axis=0, keepdims=True)
        local_max[source] = largest
        half_width = block.shape[0] // 2
        for half in range(2):
            columns = slice(half * half_width, (half + 1) * half_width)
            stat_out[source * 2 + half] = jnp.concatenate(
                [largest[:, columns], summed[:, columns]], axis=0
            )
            mine = jnp.logical_and(source == chip, core == half)

            @pl.when(mine)
            def _(columns=columns):
                stat_in[me] = jnp.concatenate([largest[:, columns], summed[:, columns]], axis=0)

            @pl.when(jnp.logical_not(mine))
            def _(half=half):
                stat_copy(source, half).start()

    def run_step(step, carry):
        @pl.when(step < chips)
        def _():
            source = index_of(source_of(step, at, grid))

            @pl.when(step > 0)
            def _():
                for part in range(len(parts)):
                    part_copy(source, 0, 0, part, chip).wait_recv()

            if chips > SEND_DEPTH:

                @pl.when(step >= SEND_DEPTH)
                def _():
                    forwards(step - SEND_DEPTH, lambda copy: copy.wait_send())

            forwards(step, lambda copy: copy.start())
            side_copy(source).start()

        @pl.when(step == 0)
        def _():
            load.wait()
            values = acc[...].astype(jnp.bfloat16)
            copies[...] = values
            wide = values.astype(jnp.float32)
            squares = jnp.sum(wide * wide, axis=1, keepdims=True) * alpha
            norms[...] = jnp.broadcast_to(squares, norms.shape)

        @pl.when(step > 0)
        def _():
            source = index_of(source_of(step - 1, at, grid))
            side_copy(source).wait_recv()
            score(source)

        return carry

    lax.fori_loop(0, chips + 1, run_step, 0)

    everyone = pl.ds(0, devices - 1)
    pltpu.make_async_copy(stat_in.at[everyone], stat_in.at[everyone], stat_recv).wait()
    maxima = stat_in[:, 0, :]
    sums = stat_in[:, 1, :]
    largest = jnp.max(maxima, axis=0, keepdims=True)
    summed = jnp.sum(sums * jnp.exp2(maxima - largest), axis=0, keepdims=True)
    own_total = largest + jnp.log(summed) * LOG2E
    totals[me] = own_total
    total_ref[...] = own_total * LN2

    def tell(index, carry):
        other = lax.rem(me + index, devices)
        pltpu.make_async_remote_copy(
            src_ref=totals.at[me],
            dst_ref=totals.at[me],
            send_sem=total_send,
            recv_sem=total_recv,
            device_id=(lax.rem(other, 2), other // 2),
            device_id_type=MESH,
        ).start()
        return carry

    lax.fori_loop(1, devices, tell, 0)
    counts[...] = jnp.zeros_like(counts)
    pltpu.make_async_copy(totals.at[everyone], totals.at[everyone], total_recv).wait()

    width = 2 * xbuf.shape[2]

    def weigh(group, carry):
        for index in range(chunk):
            source = group * chunk + index
            total = jnp.concatenate([totals[source * 2], totals[source * 2 + 1]], axis=1)
            factor = jnp.exp2(local_max[source] - total)
            part = (ebuf[source] * factor).astype(jnp.bfloat16)
            weights[:, index * width : (index + 1) * width] = part
            wide = part.astype(jnp.float32)
            counts[...] += wide[:, : width // 2] + wide[:, width // 2 :]
        block = xbuf[pl.ds(group * chunk, chunk)].reshape(chunk * width, xbuf.shape[3])
        acc[...] += jnp.dot(weights[...], block, preferred_element_type=jnp.float32)
        return carry

    lax.fori_loop(0, chips // chunk, weigh, 0)

    tiles = 4
    span = own_rows // tiles
    stores = []
    for tile in range(tiles):
        rows = pl.ds(tile * span, span)
        scale = 1.0 / (jnp.sum(counts[rows, :], axis=1, keepdims=True) + 1.0)
        acc[rows, :] = acc[rows, :] * scale
        store = pltpu.make_async_copy(acc.at[rows], out_hbm.at[rows], store_sem.at[tile])
        store.start()
        stores.append(store)

    def settle(step, carry):
        forwards(step, lambda copy: copy.wait_send())
        source = index_of(source_of(step, at, grid))
        side_copy(source).wait_send()
        return carry

    lax.fori_loop(max(0, chips - SEND_DEPTH), chips, settle, 0)
    if chips > SEND_DEPTH:

        def settle_side(step, carry):
            side_copy(index_of(source_of(step, at, grid))).wait_send()
            return carry

        lax.fori_loop(0, chips - SEND_DEPTH, settle_side, 0)
    pltpu.make_async_copy(stat_out.at[everyone], stat_out.at[everyone], stat_send).wait()
    pltpu.make_async_copy(totals.at[everyone], totals.at[everyone], total_send).wait()
    for store in stores:
        store.wait()


def on_device(chips, points, centroids):
    rows, features = points.shape
    own = centroids.shape[0]
    grid = chip_grid(chips)
    parts = row_parts(rows)
    alpha = 7.0 / math.sqrt(features) * LOG2E
    devices = 2 * chips
    chunk = 4
    links = len(parts) * sum(0 if n == 1 else (1 if n == 2 else 2) for n in grid)
    dma = pltpu.SemaphoreType.DMA
    f32, bf16 = jnp.float32, jnp.bfloat16
    new_centroids, total = pl.pallas_call(
        functools.partial(kernel, grid, parts, alpha, chunk),
        out_shape=(
            jax.ShapeDtypeStruct((own, features), f32),
            jax.ShapeDtypeStruct((1, rows), f32),
        ),
        in_specs=[pl.BlockSpec(memory_space=pltpu.VMEM), pl.BlockSpec(memory_space=pl.ANY)],
        out_specs=(pl.BlockSpec(memory_space=pl.ANY), pl.BlockSpec(memory_space=pltpu.VMEM)),
        scratch_shapes=[
            pltpu.VMEM((chips, 2, rows, features), bf16),
            pltpu.VMEM((own, features), f32),
            pltpu.VMEM((own, features), bf16),
            pltpu.VMEM((own, 2 * rows), f32),
            pltpu.VMEM((chips, own, 2 * rows), f32),
            pltpu.VMEM((own, chunk * 2 * rows), bf16),
            pltpu.VMEM((own, rows), f32),
            pltpu.VMEM((chips, 1, 2 * rows), f32),
            pltpu.VMEM((devices, 2, rows), f32),
            pltpu.VMEM((devices, 2, rows), f32),
            pltpu.VMEM((devices, 1, rows), f32),
            dma,
            dma((4,)),
            dma((SEND_DEPTH, links)),
            dma((chips, len(parts))),
            dma((chips,)),
            dma((chips,)),
            dma,
            dma,
            dma,
            dma,
        ],
        compiler_params=pltpu.CompilerParams(
            collective_id=0, has_side_effects=True, vmem_limit_bytes=60 * 1024 * 1024
        ),
        cost_estimate=pl.CostEstimate(
            flops=4 * own * devices * rows * features,
            bytes_accessed=8 * own * features,
            transcendentals=own * devices * rows,
        ),
        name="refine",
    )(points, centroids)
    return (new_centroids, total.reshape(rows))


def solution(mesh):
    placed = (P(("dp", "cent"), None), P(("dp", "cent"), None))
    return jax.shard_map(
        functools.partial(on_device, mesh.shape["cent"]),
        mesh=mesh,
        in_specs=placed,
        out_specs=(P(("dp", "cent"), None), P(("dp", "cent"))),
        check_vma=False,
    )
```

time: 242 us -> 77.1 us (0.32)
  waiting for transfers between devices: 86.2 us -> 0 us
  blocking collectives: 79.1 us -> 0 us
  Pallas kernels: 0 us -> 72 us
  matrix products: 38.3 us -> 0 us
  other arithmetic: 18.6 us -> 0 us
  between operations: 14.5 us -> 0.65 us
    all_gather x2 -> x0, waiting for transfers between devices: 80.9 us -> none  [the longest x1 66.7 us: on_device(): members = lax.all_gather(points, 'cent', axis=0, tiled=True)]
    pallas_call x0 -> x1, Pallas kernels: none -> 72 us  [on_device(): pl.pallas_call(functools.partial(kernel, grid, parts, alpha, chunk), out_...]
    pmax x1 -> x0, blocking collectives: 39.3 us -> none  [on_device(): lax.pmax(local_max.astype(jnp.bfloat16), 'cent').astype(local_max.dtype)]
    dot_general x6 -> x0, matrix products: 38.3 us -> none  [the longest x4 27.7 us: score_block(): lax.dot_general(members, cent_block, (((1,), (1,)), ((), ())), preferred_...]
    psum x1 -> x0, blocking collectives: 37.3 us -> none  [on_device(): global_sum = lax.psum(local_sum * jnp.exp(local_max - global_max), 'cent')]
    reduce_sum x3 -> x0, other arithmetic: 11.4 us -> none  [the longest x1 8.04 us: fold_stats(): jnp.sum(jnp.exp(scores - new_max[:, None]), axis=1)]
    reduce_scatter x2 -> x0, waiting for transfers between devices: 4.59 us -> none  [on_device(): lax.psum_scatter(partial_sums, 'dp', scatter_dimension=0, tiled=True)]
    div x1 -> x0, other arithmetic: 3.94 us -> none  [on_device(): new_centroids = (own_sums + centroids) / (own_counts[:, None] + 1.0)]
  transfers between devices with their start and end apart: 4 -> 0, of which waited for: 3 -> 0; matrix products, arithmetic and copies ran while one was open for 8% -> 0% of each run, Pallas kernels for 0% -> 0%
where the time goes in v1:
time: 77.1 us; the launch traced here: 76.9 us
  Pallas kernels  72 us (93%)
  local copies, waits for them, and re-layouts  4.27 us (6%)
    pallas_call x1, Pallas kernels, on_device(): pl.pallas_call(functools.partial(kernel, grid, parts, alpha, chunk), out_...  72 us
    unnamed x4, local copies, waits for them, and re-layouts  4.27 us

profile of v1, /device:TPU:0, one launch (start us, length us, event | category | flops | bytes accessed | tf_op | source)
XLA Modules:
  0.0 76.9 jit_solution(6912957826326646924)
XLA Ops:
  0.6 72.0 %refine.1 = (f32[1024,768]{1,0:T(8,128)}, f32[1,128]{1,0:T(1,128)}) custom-call(bf16[128,768]{1,0:T(8,128)(2,1)} %points_ref.1, f32[1024,768]{1,0:T(8,128)} %cent_hbm.1), custom_call_target="tpu_custom_call" | custom-call | flops 12884901888 | bytes 6291456 | tf_op jit(solution)/shard_map/refine/pallas_call | solution.py:331
  72.6 0.0 copy-start
  72.6 3.8 %copy.6 = f32[1024,768]{1,0:T(8,128)} copy(f32[1024,768]{1,0:T(8,128)} %get-tuple-element.8) | data formatting | bytes 6291456
  76.4 0.0 copy-done
  76.4 0.5 copy.7
Async XLA Ops:
  72.6 3.8 %copy-start = (f32[1,128]{1,0:T(1,128)S(1)}, f32[1,128]{1,0:T(1,128)}, u32[]{:S(2)}) copy-start(f32[1,128]{1,0:T(1,128)} %get-tuple-element.5) | copy-start | bytes 1540

commit v2 on v1

--- a/solution.py
+++ b/solution.py
@@ -13,13 +13,15 @@
 LN2 = 0.6931471805599453
 Z_AXIS, Y_AXIS, X_AXIS = 0, 1, 2
 SHARES = (
-    (0.5, (Z_AXIS, X_AXIS, Y_AXIS)),
-    (0.5, (Z_AXIS, Y_AXIS, X_AXIS)),
+    (0.375, (Z_AXIS, X_AXIS, Y_AXIS)),
+    (0.375, (Z_AXIS, Y_AXIS, X_AXIS)),
+    (0.125, (X_AXIS, Y_AXIS, Z_AXIS)),
+    (0.125, (Y_AXIS, X_AXIS, Z_AXIS)),
 )
 SEND_DEPTH = 16
 NEAREST = (
-    (0, 0, 0), (0, 0, 1), (0, 1, 0), (1, 0, 0), (0, 1, 1), (1, 0, 1), (1, 1, 0), (2, 0, 0),
-    (1, 1, 1), (2, 0, 1), (2, 1, 0), (3, 0, 0), (2, 1, 1), (3, 0, 1), (3, 1, 0), (3, 1, 1),
+    (0, 0, 0), (1, 0, 0), (0, 0, 1), (0, 1, 0), (2, 0, 0), (0, 1, 1), (1, 0, 1), (1, 1, 0),
+    (3, 0, 0), (1, 1, 1), (2, 0, 1), (2, 1, 0), (2, 1, 1), (3, 0, 1), (3, 1, 0), (3, 1, 1),
 )
 
 
@@ -130,12 +132,14 @@
     def index_of(place):
         return place[0] * strides[0] + place[1] * strides[1] + place[2]
 
-    def forwards(step, act):
+    def forwards(step, act, ready=None):
         place = source_of(step, at, grid)
         source = index_of(place)
         slot = lax.rem(step, SEND_DEPTH)
         link = 0
         for part, (_, _, order) in enumerate(parts):
+            if ready is not None:
+                ready(source, part)
             for position, axis in enumerate(order):
                 if grid[axis] == 1:
                     continue
@@ -210,9 +214,9 @@
         def _():
             source = index_of(source_of(step, at, grid))
 
-            @pl.when(step > 0)
-            def _():
-                for part in range(len(parts)):
+            def ready(source, part):
+                @pl.when(step > 0)
+                def _():
                     part_copy(source, 0, 0, part, chip).wait_recv()
 
             if chips > SEND_DEPTH:
@@ -221,7 +225,7 @@
                 def _():
                     forwards(step - SEND_DEPTH, lambda copy: copy.wait_send())
 
-            forwards(step, lambda copy: copy.start())
+            forwards(step, lambda copy: copy.start(), ready)
             side_copy(source).start()
 
         @pl.when(step == 0)

time: 77.1 us -> 70.6 us (0.916)
  Pallas kernels: 72 us -> 65.5 us
    pallas_call x1, Pallas kernels: 72 us -> 65.5 us  [on_device(): pl.pallas_call(functools.partial(kernel, grid, parts, alpha, chunk), out_...]
where the time goes in v2:
time: 70.6 us; the launch traced here: 70.4 us
  Pallas kernels  65.5 us (93%)
  local copies, waits for them, and re-layouts  4.27 us (6%)
    pallas_call x1, Pallas kernels, on_device(): pl.pallas_call(functools.partial(kernel, grid, parts, alpha, chunk), out_...  65.5 us
    unnamed x4, local copies, waits for them, and re-layouts  4.27 us

profile of v2, /device:TPU:0, one launch (start us, length us, event | category | flops | bytes accessed | tf_op | source)
XLA Modules:
  0.0 70.4 jit_solution(6323021767466897705)
XLA Ops:
  0.6 65.5 %refine.1 = (f32[1024,768]{1,0:T(8,128)}, f32[1,128]{1,0:T(1,128)}) custom-call(bf16[128,768]{1,0:T(8,128)(2,1)} %points_ref.1, f32[1024,768]{1,0:T(8,128)} %cent_hbm.1), custom_call_target="tpu_custom_call" | custom-call | flops 12884901888 | bytes 6291456 | tf_op jit(solution)/shard_map/refine/pallas_call | solution.py:335
  66.1 0.0 copy-start
  66.1 3.8 %copy.6 = f32[1024,768]{1,0:T(8,128)} copy(f32[1024,768]{1,0:T(8,128)} %get-tuple-element.8) | data formatting | bytes 6291456
  69.9 0.0 copy-done
  69.9 0.5 copy.7
Async XLA Ops:
  66.1 3.8 %copy-start = (f32[1,128]{1,0:T(1,128)S(1)}, f32[1,128]{1,0:T(1,128)}, u32[]{:S(2)}) copy-start(f32[1,128]{1,0:T(1,128)} %get-tuple-element.5) | copy-start | bytes 1540

commit v3 on v2

--- a/solution.py
+++ b/solution.py
@@ -75,10 +75,10 @@
 
 def kernel(
     grid, parts, alpha, chunk,
-    points_ref, cent_hbm, out_hbm, total_ref,
-    xbuf, acc, copies, norms, ebuf, weights, counts, local_max,
+    points_ref, cent_hbm, acc, total_ref,
+    xbuf, copies, norms, ebuf, weights, counts, local_max,
     stat_out, stat_in, totals,
-    load_sem, store_sem, send_sem, recv_sem, side_send, side_recv,
+    load_sem, send_sem, recv_sem, side_send, side_recv,
     stat_send, stat_recv, total_send, total_recv,
 ):
     nz, ny, nx = grid
@@ -91,7 +91,9 @@
     strides = (ny * nx, nx, 1)
     own_rows = copies.shape[0]
 
-    load = pltpu.make_async_copy(cent_hbm, acc, load_sem)
+    own_block = pltpu.make_async_copy(points_ref, xbuf.at[chip, core], load_sem.at[0])
+    own_block.start()
+    load = pltpu.make_async_copy(cent_hbm, acc, load_sem.at[1])
     load.start()
 
     barrier = pltpu.get_barrier_semaphore()
@@ -104,7 +106,7 @@
         return carry
 
     lax.fori_loop(1, devices, greet, 0)
-    xbuf[chip, core] = points_ref[...]
+    own_block.wait()
     pl.semaphore_wait(barrier, devices - 1)
 
     def part_copy(source, slot, link, part, target):
@@ -292,14 +294,10 @@
 
     tiles = 4
     span = own_rows // tiles
-    stores = []
     for tile in range(tiles):
         rows = pl.ds(tile * span, span)
         scale = 1.0 / (jnp.sum(counts[rows, :], axis=1, keepdims=True) + 1.0)
         acc[rows, :] = acc[rows, :] * scale
-        store = pltpu.make_async_copy(acc.at[rows], out_hbm.at[rows], store_sem.at[tile])
-        store.start()
-        stores.append(store)
 
     def settle(step, carry):
         forwards(step, lambda copy: copy.wait_send())
@@ -317,8 +315,6 @@
         lax.fori_loop(0, chips - SEND_DEPTH, settle_side, 0)
     pltpu.make_async_copy(stat_out.at[everyone], stat_out.at[everyone], stat_send).wait()
     pltpu.make_async_copy(totals.at[everyone], totals.at[everyone], total_send).wait()
-    for store in stores:
-        store.wait()
 
 
 def on_device(chips, points, centroids):
@@ -338,11 +334,10 @@
             jax.ShapeDtypeStruct((own, features), f32),
             jax.ShapeDtypeStruct((1, rows), f32),
         ),
-        in_specs=[pl.BlockSpec(memory_space=pltpu.VMEM), pl.BlockSpec(memory_space=pl.ANY)],
-        out_specs=(pl.BlockSpec(memory_space=pl.ANY), pl.BlockSpec(memory_space=pltpu.VMEM)),
+        in_specs=[pl.BlockSpec(memory_space=pltpu.HBM), pl.BlockSpec(memory_space=pltpu.HBM)],
+        out_specs=(pl.BlockSpec(memory_space=pltpu.VMEM), pl.BlockSpec(memory_space=pltpu.VMEM)),
         scratch_shapes=[
             pltpu.VMEM((chips, 2, rows, features), bf16),
-            pltpu.VMEM((own, features), f32),
             pltpu.VMEM((own, features), bf16),
             pltpu.VMEM((own, 2 * rows), f32),
             pltpu.VMEM((chips, own, 2 * rows), f32),
@@ -352,8 +347,7 @@
             pltpu.VMEM((devices, 2, rows), f32),
             pltpu.VMEM((devices, 2, rows), f32),
             pltpu.VMEM((devices, 1, rows), f32),
-            dma,
-            dma((4,)),
+            dma((2,)),
             dma((SEND_DEPTH, links)),
             dma((chips, len(parts))),
             dma((chips,)),
@@ -364,7 +358,7 @@
             dma,
         ],
         compiler_params=pltpu.CompilerParams(
-            collective_id=0, has_side_effects=True, vmem_limit_bytes=60 * 1024 * 1024
+            collective_id=0, has_side_effects=True, vmem_limit_bytes=48 * 1024 * 1024
         ),
         cost_estimate=pl.CostEstimate(
             flops=4 * own * devices * rows * features,

time: 70.6 us -> 67.6 us (0.958)
  Pallas kernels: 65.5 us -> 63.7 us
  local copies, waits for them, and re-layouts: 4.27 us -> 3.1 us
    pallas_call x1, Pallas kernels: 65.5 us -> 63.7 us  [on_device(): pl.pallas_call(functools.partial(kernel, grid, parts, alpha, chunk), out_...]
    unnamed x4, local copies, waits for them, and re-layouts: 4.27 us -> 3.1 us
where the time goes in v3:
time: 67.6 us; the launch traced here: 67.5 us
  Pallas kernels  63.7 us (94%)
  local copies, waits for them, and re-layouts  3.1 us (5%)
    pallas_call x1, Pallas kernels, on_device(): pl.pallas_call(functools.partial(kernel, grid, parts, alpha, chunk), out_...  63.7 us
    unnamed x4, local copies, waits for them, and re-layouts  3.1 us

profile of v3, /device:TPU:0, one launch (start us, length us, event | category | flops | bytes accessed | tf_op | source)
XLA Modules:
  0.0 67.5 jit_solution(4695894574343976474)
XLA Ops:
  0.6 0.0 copy-start
  0.6 0.9 %copy-done = bf16[128,768]{1,0:T(8,128)(2,1)S(1)} copy-done((bf16[128,768]{1,0:T(8,128)(2,1)S(1)}, bf16[128,768]{1,0:T(8,128)(2,1)}, u32[]{:S(2)}) %copy-start) | copy-done | bytes 196632
  1.6 63.7 %refine.1 = (f32[1024,768]{1,0:T(8,128)S(1)}, f32[1,128]{1,0:T(1,128)S(1)}) custom-call(bf16[128,768]{1,0:T(8,128)(2,1)S(1)} %copy-done, f32[1024,768]{1,0:T(8,128)} %cent_hbm.1), custom_call_target="tpu_custom_call" | custom-call | flops 12884901888 | bytes 6291456 | tf_op jit(solution)/shard_map/refine/pallas_call | solution.py:331
  65.3 1.7 %copy.6 = f32[1024,768]{1,0:T(8,128)} copy(f32[1024,768]{1,0:T(8,128)S(1)} %get-tuple-element.8) | data formatting | bytes 6291456
  67.0 0.5 copy.7
Async XLA Ops:
  0.6 0.9 %copy-start = (bf16[128,768]{1,0:T(8,128)(2,1)S(1)}, bf16[128,768]{1,0:T(8,128)(2,1)}, u32[]{:S(2)}) copy-start(bf16[128,768]{1,0:T(8,128)(2,1)} %points_ref.1) | copy-start | bytes 589828

commit v4 on v3

--- a/solution.py
+++ b/solution.py
@@ -13,10 +13,8 @@
 LN2 = 0.6931471805599453
 Z_AXIS, Y_AXIS, X_AXIS = 0, 1, 2
 SHARES = (
-    (0.375, (Z_AXIS, X_AXIS, Y_AXIS)),
-    (0.375, (Z_AXIS, Y_AXIS, X_AXIS)),
-    (0.125, (X_AXIS, Y_AXIS, Z_AXIS)),
-    (0.125, (Y_AXIS, X_AXIS, Z_AXIS)),
+    (0.5, (Z_AXIS, X_AXIS, Y_AXIS)),
+    (0.5, (Z_AXIS, Y_AXIS, X_AXIS)),
 )
 SEND_DEPTH = 16
 NEAREST = (
@@ -239,15 +237,15 @@
             squares = jnp.sum(wide * wide, axis=1, keepdims=True) * alpha
             norms[...] = jnp.broadcast_to(squares, norms.shape)
 
-        @pl.when(step > 0)
+        @pl.when(step > 1)
         def _():
-            source = index_of(source_of(step - 1, at, grid))
+            source = index_of(source_of(step - 2, at, grid))
             side_copy(source).wait_recv()
             score(source)
 
         return carry
 
-    lax.fori_loop(0, chips + 1, run_step, 0)
+    lax.fori_loop(0, chips + 2, run_step, 0)
 
     everyone = pl.ds(0, devices - 1)
     pltpu.make_async_copy(stat_in.at[everyone], stat_in.at[everyone], stat_recv).wait()
@@ -324,7 +322,7 @@
     parts = row_parts(rows)
     alpha = 7.0 / math.sqrt(features) * LOG2E
     devices = 2 * chips
-    chunk = 4
+    chunk = 8
     links = len(parts) * sum(0 if n == 1 else (1 if n == 2 else 2) for n in grid)
     dma = pltpu.SemaphoreType.DMA
     f32, bf16 = jnp.float32, jnp.bfloat16

time: 67.6 us -> 65.2 us (0.964)
  Pallas kernels: 63.7 us -> 61.3 us
    pallas_call x1, Pallas kernels: 63.7 us -> 61.3 us  [on_device(): pl.pallas_call(functools.partial(kernel, grid, parts, alpha, chunk), out_...]
where the time goes in v4:
time: 65.2 us; the launch traced here: 65.1 us
  Pallas kernels  61.3 us (94%)
  local copies, waits for them, and re-layouts  3.1 us (5%)
    pallas_call x1, Pallas kernels, on_device(): pl.pallas_call(functools.partial(kernel, grid, parts, alpha, chunk), out_...  61.3 us
    unnamed x4, local copies, waits for them, and re-layouts  3.1 us

profile of v4, /device:TPU:0, one launch (start us, length us, event | category | flops | bytes accessed | tf_op | source)
XLA Modules:
  0.0 65.1 jit_solution(3247728417447079086)
XLA Ops:
  0.6 0.0 copy-start
  0.6 0.9 %copy-done = bf16[128,768]{1,0:T(8,128)(2,1)S(1)} copy-done((bf16[128,768]{1,0:T(8,128)(2,1)S(1)}, bf16[128,768]{1,0:T(8,128)(2,1)}, u32[]{:S(2)}) %copy-start) | copy-done | bytes 196632
  1.6 61.3 %refine.1 = (f32[1024,768]{1,0:T(8,128)S(1)}, f32[1,128]{1,0:T(1,128)S(1)}) custom-call(bf16[128,768]{1,0:T(8,128)(2,1)S(1)} %copy-done, f32[1024,768]{1,0:T(8,128)} %cent_hbm.1), custom_call_target="tpu_custom_call" | custom-call | flops 12884901888 | bytes 6291456 | tf_op jit(solution)/shard_map/refine/pallas_call | solution.py:329
  62.9 1.7 %copy.6 = f32[1024,768]{1,0:T(8,128)} copy(f32[1024,768]{1,0:T(8,128)S(1)} %get-tuple-element.8) | data formatting | bytes 6291456
  64.6 0.5 copy.7
Async XLA Ops:
  0.6 0.9 %copy-start = (bf16[128,768]{1,0:T(8,128)(2,1)S(1)}, bf16[128,768]{1,0:T(8,128)(2,1)}, u32[]{:S(2)}) copy-start(bf16[128,768]{1,0:T(8,128)(2,1)} %points_ref.1) | copy-start | bytes 589828
